TPU v7x, 256 devices: a whole 4x4x8 slice. The times are simulated.
256 devices in a mesh: ctx: 32 (over y, z), dp: 8 (over x, core).
Axes of the slice: x: 4, y: 4, z: 8, core: 2. Of those that a mesh axis runs over, the one named last changes fastest.
Arguments:
- queries: bfloat16 [4096, 4, 8192], P(('ctx', 'dp')), may hold values from -88 to 88
- new_kv: bfloat16 [4096, 4, 2048], P(('ctx', 'dp')), may hold values from -4 to 4
- kv_pages: bfloat16 [8192, 64, 2048], P(('ctx', 'dp')), may hold values from -6 to 6
- page_owner: int32 [8192, 1], P(('ctx', 'dp')), may hold values from 0 to 31; in each aligned block of 32 rows (0 to 31, 32 to 63, ...) at most 2 rows name the same one
- page_request: int32 [8192], P(('ctx', 'dp')), may hold values from 0 to 15
- page_fill: int32 [8192], P(('ctx', 'dp')), may hold values from 1 to 64
- prefix_kv: bfloat16 [512, 2048], P(('ctx', 'dp')), may hold values from -6 to 6
- prefix_use: int32 [4096], P(('ctx', 'dp')), may hold values 0 or 1
Outputs:
- attention: bfloat16 [4096, 4, 8192], P(('ctx', 'dp'))
Inputs may be any that keep to these rules, and one draw needn't show every extreme that they name: `page_owner`: among one device's pages at most 2 name the same owner, and in some device's pages one owner is named exactly 2 times.
All inputs are finite; a program needn't handle non-finite values. No bound on the sum of `prefix_use` on one device may be relied on, other than what follows from the above.
Results may differ from a plain program's by a relative error of at most 0.0045.
Values may be sent and summed in bfloat16 or wider, within the bound.
A program may use at most 128 MiB of HBM per device.

v0:
```python
import math

import jax
import jax.numpy as jnp
from jax import lax
from jax.sharding import PartitionSpec as P

KVH = 8
HD = 128
G = 8


masked_score = -1e30


def finish_group(scores, visible, value_rows, form):
    scores = jnp.where(visible, scores, masked_score)
    highest = jnp.max(scores, axis=-1)
    weights = jnp.where(visible, jnp.exp(scores - highest[..., None]), 0.0).astype(jnp.bfloat16)
    totals = jnp.sum(weights, axis=-1, dtype=jnp.float32)
    output = jnp.einsum(form, weights, value_rows, preferred_element_type=jnp.float32)
    return (highest, totals, output)


def slot_attend(query_rows, page_rows, fills):
    slot_count, page_len, channels = page_rows.shape
    step_count = query_rows.shape[1]
    width = KVH * HD
    split_rows = query_rows.reshape(slot_count, step_count, KVH, G, HD)
    key_rows = page_rows[:, :, :width].reshape(slot_count, page_len, KVH, HD)
    value_rows = page_rows[:, :, width:].reshape(slot_count, page_len, KVH, HD)
    scores = jnp.einsum(
        "sqkgd,stkd->skqgt", split_rows, key_rows, preferred_element_type=jnp.float32
    )
    scores = scores * (1.0 / math.sqrt(HD))
    visible = (jnp.arange(page_len, dtype=jnp.int32)[None, :] < fills[:, None])[
        :, None, None, None, :
    ]
    return finish_group(scores, visible, value_rows, "skqgt,stkd->skqgd")


def body(queries, new_kv, kv_pages, page_owner, page_request, page_fill, prefix_kv, prefix_use):
    ctx_size = lax.axis_size("ctx")
    pages_dev, page_len, channels = kv_pages.shape
    request_count, step_count, query_width = queries.shape
    width = KVH * HD
    capacity = 2 * pages_dev // ctx_size
    slots = ctx_size * capacity
    owners = page_owner[:, 0]
    owner_hot = (owners[:, None] == jnp.arange(ctx_size, dtype=jnp.int32)[None, :]).astype(
        jnp.int32
    )
    earlier = jnp.cumsum(owner_hot, axis=0) - owner_hot
    position = jnp.sum(earlier * owner_hot, axis=1)
    slot_of_page = owners * capacity + position
    matches = (slot_of_page[None, :] == jnp.arange(slots, dtype=jnp.int32)[:, None]).astype(
        jnp.int32
    )
    present = jnp.sum(matches, axis=1)
    page_of_slot = jnp.sum(matches * jnp.arange(pages_dev, dtype=jnp.int32)[None, :], axis=1)
    send_request = jnp.where(present > 0, jnp.sum(matches * page_request[None, :], axis=1), -1)
    send_fill = jnp.sum(matches * page_fill[None, :], axis=1)
    meta_rows = jnp.stack([send_request, send_fill], axis=-1).reshape(ctx_size, capacity, 2)
    arrived_meta = lax.all_to_all(
        meta_rows, "ctx", split_axis=0, concat_axis=0, tiled=True
    ).reshape(slots, 2)
    slot_request = arrived_meta[:, 0]
    slot_fill = arrived_meta[:, 1]
    local_pages = jnp.take(kv_pages, page_of_slot, axis=0)
    asked_rows = jnp.take(queries, jnp.maximum(slot_request, 0), axis=0)
    arrived = lax.all_to_all(
        local_pages.reshape(ctx_size, capacity, page_len, channels),
        "ctx",
        split_axis=0,
        concat_axis=0,
        tiled=True,
    ).reshape(slots, page_len, channels)
    slot_max, slot_sum, slot_out = slot_attend(asked_rows, arrived, slot_fill)
    split_rows = queries.reshape(request_count, step_count, KVH, G, HD)
    scaling = 1.0 / math.sqrt(HD)
    prefix_all = lax.all_gather(prefix_kv, ("ctx", "dp"), axis=0, tiled=True)
    prefix_len = prefix_all.shape[0]
    prefix_keys = prefix_all[:, :width].reshape(prefix_len, KVH, HD)
    prefix_values = prefix_all[:, width:].reshape(prefix_len, KVH, HD)
    scores = (
        jnp.einsum("rqkgd,tkd->rkqgt", split_rows, prefix_keys, preferred_element_type=jnp.float32)
        * scaling
    )
    everywhere = jnp.ones((1, 1, 1, 1, prefix_len), dtype=bool)
    prefix_max, prefix_sum, prefix_out = finish_group(
        scores, everywhere, prefix_values, "rkqgt,tkd->rkqgd"
    )
    reads = (prefix_use > 0)[:, None, None, None]
    prefix_max = jnp.where(reads, prefix_max, masked_score)
    prefix_sum = jnp.where(reads, prefix_sum, 0.0)
    prefix_out = jnp.where(reads[..., None], prefix_out, 0.0)
    fresh_keys = new_kv[:, :, :width].reshape(request_count, step_count, KVH, HD)
    fresh_values = new_kv[:, :, width:].reshape(request_count, step_count, KVH, HD)
    scores = (
        jnp.einsum("rqkgd,rtkd->rkqgt", split_rows, fresh_keys, preferred_element_type=jnp.float32)
        * scaling
    )
    causal = (jnp.arange(step_count)[None, :] <= jnp.arange(step_count)[:, None])[
        None, None, :, None, :
    ]
    fresh_max, fresh_sum, fresh_out = finish_group(
        scores, causal, fresh_values, "rkqgt,rtkd->rkqgd"
    )
    owned = (slot_request[None, :] == jnp.arange(request_count, dtype=jnp.int32)[:, None]).astype(
        jnp.float32
    )
    page_best = jnp.max(
        jnp.where(owned[:, :, None, None, None] > 0, slot_max[None], masked_score), axis=1
    )
    overall = jnp.maximum(jnp.maximum(page_best, prefix_max), fresh_max)
    overall_slot = jnp.einsum("rs,rkqg->skqg", owned, overall, precision=lax.Precision.HIGHEST)
    slot_factor = jnp.exp(slot_max - overall_slot)
    prefix_factor = jnp.exp(prefix_max - overall)
    fresh_factor = jnp.exp(fresh_max - overall)
    totals = jnp.einsum(
        "rs,skqg->rkqg", owned, slot_factor * slot_sum, precision=lax.Precision.HIGHEST
    )
    totals = totals + prefix_factor * prefix_sum + fresh_factor * fresh_sum
    output = jnp.einsum(
        "rs,skqgd->rkqgd", owned, slot_factor[..., None] * slot_out, precision=lax.Precision.HIGHEST
    )
    output = output + prefix_factor[..., None] * prefix_out + fresh_factor[..., None] * fresh_out
    output = output / totals[..., None]
    output = jnp.transpose(output, (0, 2, 1, 3, 4)).reshape(request_count, step_count, query_width)
    return output.astype(jnp.bfloat16)


def solution(mesh):
    placed = (
        P(("ctx", "dp"), None, None),
        P(("ctx", "dp"), None, None),
        P(("ctx", "dp"), None, None),
        P(("ctx", "dp"), None),
        P(("ctx", "dp")),
        P(("ctx", "dp")),
        P(("ctx", "dp"), None),
        P(("ctx", "dp")),
    )
    return jax.shard_map(
        body, mesh=mesh, in_specs=placed, out_specs=P(("ctx", "dp"), None, None), check_vma=False
    )
```

profile of v0, /device:TPU:185, one launch (start us, length us, event | category | flops | bytes accessed | tf_op | source)
XLA Modules:
  0.0 561.3 jit_solution(1716831268912241659)
XLA Ops:
  7.3 0.8 select_reduce_fusion.4
  10.5 8.7 %all-to-all-start = ((s32[32,2,2]{1,2,0:T(2,128)}), s32[32,2,2]{1,2,0:T(2,128)S(1)}, u32[]{:S(2)}, u32[]{:S(2)}) async-start(s32[32,2,2]{1,2,0:T(2,128)} %copy.95), calls=%async_computation | async-start | bytes 65536 | tf_op jit(solution)/shard_map/all_to_all | solution.py:64
  19.3 10.8 %gather_fusion.1 = bf16[64,64,2048]{2,1,0:T(8,128)(2,1)} fusion(bf16[32,64,2048]{2,1,0:T(8,128)(2,1)} %param.10, s32[1024]{0:T(1024)S(1)} %pad_clamp_fusion), kind=kCustom, calls=%fused_computation.1 | custom fusion | bytes 33554688 | tf_op jit(solution)/shard_map/jit(_take)/gather | solution.py:69
  30.1 14.2 %broadcast_select_fusion = bf16[32,2,64,2048]{3,2,1,0:T(8,128)(2,1)} fusion(bf16[32,2,64,2048]{3,2,1,0:T(8,128)(2,1)} %bitcast.146, pred[32,2]{1,0:T(8,128)(4,1)S(1)} %compare_and_fusion), kind=kLoop, calls=%fused_computation.2 | loop fusion | flops 8388608 | bytes 33554496 | tf_op jit(solution)/shard_map/jit(_take)/select_n | solution.py:69
  44.4 9.4 %all-to-all-start.1 = ((bf16[32,2,64,2048]{3,2,1,0:T(8,128)(2,1)}), bf16[32,2,64,2048]{3,2,1,0:T(8,128)(2,1)}, u32[]{:S(2)}, u32[]{:S(2)}) async-start(bf16[32,2,64,2048]{3,2,1,0:T(8,128)(2,1)} %broadcast_select_fusion), calls=%async_computation.1 | async-start | bytes 33554432 | tf_op jit(solution)/shard_map/all_to_all | solution.py:71
  54.5 1.1 reshape.181
  55.7 5.9 %fusion.50 = (f32[16,8,4,8]{3,2,1,0:T(4,128)S(1)}, f32[16,8,4,8,4]{3,4,2,1,0:T(4,128)S(1)}) fusion(bf16[16,4,2048]{2,1,0:T(4,128)(2,1)} %param.9, bf16[16,4,8,8,128]{4,3,2,1,0:T(8,128)(2,1)S(1)} %reshape.181, pred[4,4]{1,0:T(4,128)(4,1)S(1)} %iota_compare_fusion.6), kind=kOutput, calls=%fused_computation.93 | convolution fusion | flops 4239360 | bytes 1261584 | tf_op jit(solution)/shard_map/rqkgd,rtkd->rkqgt/dot_general | solution.py:100
  61.7 1.0 convert_reduce_fusion.2
  63.0 3.0 fusion.25
  66.1 6.3 %gather_fusion = bf16[64,4,8192]{2,1,0:T(4,128)(2,1)} fusion(bf16[16,4,8192]{2,1,0:T(4,128)(2,1)S(1)} %copy-done, s32[1024]{0:T(1024)S(1)} %pad_clamp_fusion.1), kind=kCustom, calls=%fused_computation | custom fusion | bytes 8388864 | tf_op jit(solution)/shard_map/jit(_take)/gather | solution.py:70
  72.3 8.4 %gather.13 = bf16[64,4,8,8,128]{4,3,2,1,0:T(8,128)(2,1)} reshape(bf16[64,4,8192]{2,1,0:T(4,128)(2,1)} %gather_fusion) | data formatting | bytes 8388608 | tf_op jit(solution)/shard_map/jit(_take)/gather | solution.py:70
  80.8 174.9 %all-gather.3.cloned.1.call-done = bf16[256,2,2048]{2,1,0:T(2,128)(2,1)} async-done(((bf16[1,2,2048]{2,1,0:T(2,128)(2,1)}), bf16[256,2,2048]{2,1,0:T(2,128)(2,1)}) %all-gather.3.cloned.1.call-update) | async-done | bytes 2097168 | tf_op jit(solution)/shard_map/all_gather | solution.py:81
  255.8 2.7 reshape.203
  258.5 1.2 fusion.49
  259.7 1.5 copy.100
  261.7 2.7 bitcast_reduce_fusion
  264.5 2.3 convert_reduce_fusion
  266.8 2.9 fusion.23
  269.6 196.9 %all-to-all-done.1 = bf16[32,2,64,2048]{3,2,1,0:T(8,128)(2,1)} async-done(((bf16[32,2,64,2048]{3,2,1,0:T(8,128)(2,1)}), bf16[32,2,64,2048]{3,2,1,0:T(8,128)(2,1)}, u32[]{:S(2)}, u32[]{:S(2)}) %all-to-all-start.1) | async-done | bytes 16777248 | tf_op jit(solution)/shard_map/all_to_all | solution.py:71
  466.5 12.1 %fusion.48 = (bf16[64,64,1024]{2,1,0:T(8,128)(2,1)}, bf16[64,64,1024]{2,1,0:T(8,128)(2,1)}) fusion(bf16[64,64,2048]{2,1,0:T(8,128)(2,1)} %bitcast.10), kind=kLoop, calls=%fused_computation.91 | loop fusion | bytes 33554432 | tf_op jit(solution)/shard_map/slice | solution.py:31
  478.6 8.8 %copy.140 = bf16[512,8,8,128]{3,2,1,0:T(8,128)(2,1)} copy(bf16[512,8,8,128]{3,1,2,0:T(8,128)(2,1)} %bitcast.150) | data formatting | bytes 16777216
  487.4 7.6 %bitcast_bitcast_fusion.1 = bf16[64,64,8,128,1]{3,2,1,0,4:T(8,128)(2,1)} fusion(bf16[64,64,8,128]{3,2,1,0:T(8,128)(2,1)} %bitcast.147), kind=kLoop, calls=%fused_computation.4 | loop fusion | bytes 16777216 | tf_op jit(solution)/shard_map/reshape | solution.py:30
  494.9 12.8 %fusion.8 = (f32[64,8,4,8]{3,2,1,0:T(4,128)S(1)}, f32[64,8,4,8,64]{4,3,2,1,0:T(8,128)}) fusion(pred[64,64]{1,0:T(8,128)(4,1)S(1)} %iota_compare_fusion, bf16[64,64,8,128,1]{3,2,1,0,4:T(8,128)(2,1)} %bitcast_bitcast_fusion.1, bf16[64,4,8,8,128]{4,3,2,1,0:T(8,128)(2,1)} %gather.13, pred[64]{0:T(512)(128)(4,1)S(1)} %compare_bitcast_fusion), kind=kOutput, calls=%fused_computation.19 | convolution fusion | flops 273661952 | bytes 16846912 | tf_op jit(solution)/shard_map/sqkgd,stkd->skqgt/dot_general | solution.py:32
  507.8 0.8 copy.106
  508.6 7.4 %convert_reduce_fusion.1 = f32[64,8,4,8]{3,2,1,0:T(4,128)S(1)} fusion(f32[64,8,4,8]{3,2,1,0:T(4,128)S(1)} %get-tuple-element.25, f32[64,8,4,8,64]{4,3,2,1,0:T(8,128)} %get-tuple-element.26, pred[64,64]{1,0:T(8,128)(4,1)S(1)} %iota_compare_fusion), kind=kLoop, calls=%fused_computation.16 | loop fusion | flops 7323648 | bytes 4329472 | tf_op jit(solution)/shard_map/reduce_sum | solution.py:20
  516.8 0.8 select_reduce_fusion
  518.3 1.1 copy.107
  519.5 8.8 %copy.141 = bf16[512,8,8,128]{3,2,1,0:T(8,128)(2,1)} copy(bf16[512,8,8,128]{3,1,2,0:T(8,128)(2,1)} %bitcast.149) | data formatting | bytes 16777216
  528.2 7.6 %bitcast_bitcast_fusion = bf16[64,64,8,128,1]{3,2,1,0,4:T(8,128)(2,1)} fusion(bf16[64,64,8,128]{3,2,1,0:T(8,128)(2,1)} %bitcast.148), kind=kLoop, calls=%fused_computation.3 | loop fusion | bytes 16777216 | tf_op jit(solution)/shard_map/reshape | solution.py:31
  535.8 8.9 %broadcast_multiply_fusion = f32[64,8,4,8,128]{4,3,2,1,0:T(8,128)S(1)} fusion(f32[64,8,4,8]{3,2,1,0:T(4,128)S(1)} %copy.107, bf16[64,64,8,128,1]{3,2,1,0,4:T(8,128)(2,1)} %bitcast_bitcast_fusion, f32[64,8,4,8,64]{4,3,2,1,0:T(8,128)} %get-tuple-element.26, f32[64,8,4,8]{3,2,1,0:T(4,128)S(1)} %get-tuple-element.25, pred[64,64]{1,0:T(8,128)(4,1)S(1)} %iota_compare_fusion), kind=kOutput, calls=%fused_computation.21 | convolution fusion | flops 275775488 | bytes 21106688 | tf_op jit(solution)/shard_map/skqgt,stkd->skqgd/dot_general | solution.py:21
  544.9 8.2 %fusion.14 = bf16[16,4,8,8,128]{4,0,3,1,2:T(8,128)(2,1)S(1)} fusion(f32[16,8,4,8,128]{4,3,2,1,0:T(8,128)S(1)} %copy-done.1, f32[8,16,4,8,128]{4,1,3,2,0:T(8,128)S(1)} %copy-done.2, f32[64,8,4,8,128]{4,3,2,1,0:T(8,128)S(1)} %broadcast_multiply_fusion, f32[16,4,8,8]{0,3,1,2:T(8,128)S(1)} %get-tuple-element.9, f32[16,4,8,8]{0,3,1,2:T(8,128)S(1)} %get-tuple-element.11, ...), kind=kOutput, calls=%fused_computation.26 | convolution fusion | flops 406324224 | bytes 13680912 | tf_op jit(solution)/shard_map/rs,skqgd->rkqgd/dot_general | solution.py:124
  553.4 1.1 reshape.215
  (46 shorter events, 6.8 us)
Async XLA Ops:
  10.5 33.9 %all-to-all-start = ((s32[32,2,2]{1,2,0:T(2,128)}), s32[32,2,2]{1,2,0:T(2,128)S(1)}, u32[]{:S(2)}, u32[]{:S(2)}) async-start(s32[32,2,2]{1,2,0:T(2,128)} %copy.95), calls=%async_computation | async-start | bytes 65536 | tf_op jit(solution)/shard_map/all_to_all | solution.py:64
  44.4 10.2 %copy-start = (bf16[16,4,8192]{2,1,0:T(4,128)(2,1)S(1)}, bf16[16,4,8192]{2,1,0:T(4,128)(2,1)}, u32[]{:S(2)}) copy-start(bf16[16,4,8192]{2,1,0:T(4,128)(2,1)} %param.8) | copy-start | bytes 3145732
  44.4 18.6 %copy-start.4 = (s32[16]{0:T(128)S(1)}, s32[16]{0:T(128)}, u32[]{:S(2)}) copy-start(s32[16]{0:T(128)} %param.15) | copy-start | bytes 196
  44.4 422.1 %all-to-all-start.1 = ((bf16[32,2,64,2048]{3,2,1,0:T(8,128)(2,1)}), bf16[32,2,64,2048]{3,2,1,0:T(8,128)(2,1)}, u32[]{:S(2)}, u32[]{:S(2)}) async-start(bf16[32,2,64,2048]{3,2,1,0:T(8,128)(2,1)} %broadcast_select_fusion), calls=%async_computation.1 | async-start | bytes 33554432 | tf_op jit(solution)/shard_map/all_to_all | solution.py:71
  53.8 202.0 %all-gather.3.cloned.1.call-start = ((), (), s32[]{:S(2)}) async-start(), calls=%async_computation.2 | async-start | bytes 2105344 | tf_op jit(solution)/shard_map/all_gather | solution.py:81
  55.7 5.9 %copy-start.3 = (bf16[16,4,8,8,128]{4,3,2,1,0:T(8,128)(2,1)}, bf16[16,4,8,8,128]{4,3,2,1,0:T(8,128)(2,1)S(1)}, u32[]{:S(2)}) copy-start(bf16[16,4,8,8,128]{4,3,2,1,0:T(8,128)(2,1)S(1)} %reshape.181) | copy-start | bytes 3145732
  535.8 9.0 %copy-start.1 = (f32[16,8,4,8,128]{4,3,2,1,0:T(8,128)S(1)}, f32[16,8,4,8,128]{4,3,2,1,0:T(8,128)}, u32[]{:S(2)}) copy-start(f32[16,8,4,8,128]{4,3,2,1,0:T(8,128)} %fusion.25) | copy-start | bytes 6291460
  535.8 9.0 %copy-start.2 = (f32[8,16,4,8,128]{4,1,3,2,0:T(8,128)S(1)}, f32[8,16,4,8,128]{4,1,3,2,0:T(8,128)}, u32[]{:S(2)}) copy-start(f32[8,16,4,8,128]{4,1,3,2,0:T(8,128)} %fusion.23) | copy-start | bytes 6291460
Sparse Core Ops, SparseCore 0:
  58.4 197.3 all-gather.2
where the time goes:
time: 562 us; the launch traced here: 561 us
  waiting for transfers between devices  372 us (66%)
  local copies, waits for them, and re-layouts  83.1 us (15%)
  matrix products  44.8 us (8%)
  other arithmetic  29.1 us (5%)
  starting transfers between devices  18.4 us (3%)
  between operations  13.7 us (2%)
    all_to_all x1, waiting for transfers between devices, body(): lax.all_to_all(local_pages.reshape(ctx_size, capacity, page_len, channels...  197 us
    all_gather x1, waiting for transfers between devices, body(): prefix_all = lax.all_gather(prefix_kv, ('ctx', 'dp'), axis=0, tiled=True)  175 us
    unnamed x13, local copies, waits for them, and re-layouts  20.3 us
    dot_general x3, matrix products, finish_group(): jnp.einsum(form, weights, value_rows, preferred_element_type=jnp.float32)  14.8 us
    gather x2, local copies, waits for them, and re-layouts, body(): asked_rows = jnp.take(queries, jnp.maximum(slot_request, 0), axis=0)  14.7 us
    select_n x2, other arithmetic, body(): local_pages = jnp.take(kv_pages, page_of_slot, axis=0)  14.2 us
    dot_general x1, matrix products, slot_attend(): jnp.einsum('sqkgd,stkd->skqgt', split_rows, key_rows, preferred_element_t...  12.8 us
    slice x1, local copies, waits for them, and re-layouts, slot_attend(): value_rows = page_rows[:, :, width:].reshape(slot_count, page_len, KVH, HD)  12.1 us
  transfers between devices with their start and end apart: 3, of which 2 were waited for; matrix products, arithmetic and copies ran while one was open for 12% of the time, Pallas kernels for 0%

commit v1 on v0

v1 whole, which is shorter than its diff:
```python
import functools
import math

import jax
import jax.numpy as jnp
from jax import lax
from jax.experimental import pallas as pl
from jax.experimental.pallas import tpu as pltpu
from jax.sharding import PartitionSpec as P

KVH = 8
HD = 128
G = 8
LOW = -1e30
NY, NZ = 4, 8
NCTX = NY * NZ
NDP = 8
MESH = pl.DeviceIdType.MESH
SCALE = 1.0 / math.sqrt(HD)


def lane_head(rows):
    return lax.broadcasted_iota(jnp.int32, (rows, 128), 1) // 32


def spread(block, rows):
    head = lane_head(rows)
    zero = jnp.zeros_like(block)
    return jnp.concatenate([jnp.where(head == k, block, zero) for k in range(4)], axis=0)


def scores_half(keys, qt):
    s = lax.dot_general(
        keys, spread(qt, HD), (((1,), (0,)), ((), ())), preferred_element_type=jnp.float32
    )
    return s * SCALE


def values_half(values, w):
    stacked = jnp.concatenate(values, axis=0)
    return lax.dot_general(
        stacked,
        spread(w, w.shape[0]),
        (((0,), (0,)), ((), ())),
        preferred_element_type=jnp.float32,
    )


def group_half(keys, values, qt, visible):
    s = scores_half(keys, qt)
    if visible is not None:
        s = jnp.where(visible, s, LOW)
    m = jnp.max(s, axis=0, keepdims=True)
    w = jnp.exp(s - m)
    if visible is not None:
        w = jnp.where(visible, w, 0.0)
    w = w.astype(jnp.bfloat16)
    l = jnp.sum(w.astype(jnp.float32), axis=0, keepdims=True)
    return m, l, values_half(values, w)


def kernel(
    req, page_of, fill_of, use,
    qt_ref, pages_ref, fresh_ref, prefix_ref,
    out_ref,
    sendq, recvq, sendp, recvp, sendl, recvl,
    acc, big, tot, pre1, pre2, pre3, pre4,
    sq_sem, rq_sem, sp_sem, rp_sem, sl_sem, rl_sem, s1_sem, r1_sem, s2_sem, r2_sem, loc_sem,
):
    me = lax.axis_index("ctx")
    col = lax.axis_index("dp")
    y, z = me // NZ, me % NZ

    def ahead(i):
        return ((y + i // NZ) % NY) * NZ + (z + i % NZ) % NZ

    def behind(i):
        return ((y + NY - i // NZ) % NY) * NZ + (z + NZ - i % NZ) % NZ

    barrier = pltpu.get_barrier_semaphore()

    def greet(i, c):
        pl.semaphore_signal(barrier, inc=1, device_id={"ctx": ahead(i)}, device_id_type=MESH)
        return c

    lax.fori_loop(1, NCTX, greet, 0)

    def greet_dp(i, c):
        pl.semaphore_signal(barrier, inc=1, device_id={"dp": (col + i) % NDP}, device_id_type=MESH)
        return c

    lax.fori_loop(1, NDP, greet_dp, 0)
    pl.semaphore_wait(barrier, NCTX + NDP - 2)

    def pre_copy(i):
        return pltpu.make_async_remote_copy(
            src_ref=prefix_ref, dst_ref=pre1.at[i], send_sem=s1_sem.at[i], recv_sem=r1_sem.at[i],
            device_id={"ctx": ahead(i)}, device_id_type=MESH)

    def pre_start(i, c):
        pre_copy(i).start()
        return c

    lax.fori_loop(1, NCTX, pre_start, 0)
    pre1[0] = prefix_ref[...]

    def q_copy(i):
        return pltpu.make_async_remote_copy(
            src_ref=sendq.at[i], dst_ref=recvq.at[i], send_sem=sq_sem.at[i], recv_sem=rq_sem.at[i],
            device_id={"ctx": ahead(i)}, device_id_type=MESH)

    def gather(i, d):
        for s in range(2):
            r = jnp.maximum(req[2 * d + s], 0)
            sendq[i, s] = qt_ref[r]

    def q_start(i, c):
        gather(i, ahead(i))
        q_copy(i).start()
        return c

    lax.fori_loop(1, NCTX, q_start, 0)
    gather(0, me)

    def pre_wait(i, c):
        pre_copy(i).wait()
        return c

    lax.fori_loop(1, NCTX, pre_wait, 0)

    def pre2_copy(i):
        return pltpu.make_async_remote_copy(
            src_ref=pre1, dst_ref=pre2.at[i], send_sem=s2_sem.at[i], recv_sem=r2_sem.at[i],
            device_id={"dp": (col + i) % NDP}, device_id_type=MESH)

    def pre2_start(i, c):
        pre2_copy(i).start()
        return c

    lax.fori_loop(1, NDP, pre2_start, 0)
    pre2[0] = pre1[...]

    def fresh(r, c):
        t = lax.broadcasted_iota(jnp.int32, (16, 128), 0)
        step = lax.broadcasted_iota(jnp.int32, (16, 128), 1) % 4
        visible = t <= step
        for h in range(2):
            ln = pl.ds(h * 128, 128)
            keys = fresh_ref[r, :, pl.ds(h * 512, 512)]
            values = [fresh_ref[r, :, pl.ds(1024 + (4 * h + k) * 128, 128)] for k in range(4)]
            m, l, o = group_half(keys, values, qt_ref[r, :, ln], visible)
            big[r, :, ln] = m
            tot[r, :, ln] = l
            acc[r, :, ln] = o
        return c

    lax.fori_loop(0, 16, fresh, 0)

    def attend(src, i, o, dst_o, dst_l):
        for s in range(2):
            p = page_of[2 * o + s]
            f = fill_of[2 * o + s]
            visible = lax.broadcasted_iota(jnp.int32, (64, 128), 0) < f
            for h in range(2):
                ln = pl.ds(h * 128, 128)
                keys = pages_ref[p, :, pl.ds(h * 512, 512)]
                values = [pages_ref[p, :, pl.ds(1024 + (4 * h + k) * 128, 128)] for k in range(4)]
                m, l, out = group_half(keys, values, src[i, s, :, ln], visible)
                dst_o[i, s, :, ln] = (out * (1.0 / l)).astype(jnp.bfloat16)
                dst_l[i, pl.ds(s, 1), ln] = m + jnp.log(l)

    attend(sendq, 0, me, recvp, recvl)

    def p_copy(i):
        return pltpu.make_async_remote_copy(
            src_ref=sendp.at[i], dst_ref=recvp.at[i], send_sem=sp_sem.at[i], recv_sem=rp_sem.at[i],
            device_id={"ctx": behind(i)}, device_id_type=MESH)

    def l_copy(i):
        return pltpu.make_async_remote_copy(
            src_ref=sendl.at[i], dst_ref=recvl.at[i], send_sem=sl_sem.at[i], recv_sem=rl_sem.at[i],
            device_id={"ctx": behind(i)}, device_id_type=MESH)

    def answer(i, c):
        q_copy(i).wait()
        attend(recvq, i, behind(i), sendp, sendl)
        l_copy(i).start()
        p_copy(i).start()
        return c

    lax.fori_loop(1, NCTX, answer, 0)

    def pre2_wait(i, c):
        pre2_copy(i).wait()
        return c

    lax.fori_loop(1, NDP, pre2_wait, 0)

    def widen(i, c):
        pre3[...] = pre2[i].astype(jnp.float32).reshape(NCTX * 32, 128)
        for ch in range(16):
            pre4[ch, pl.ds(pl.multiple_of(i * 2 * NCTX, 2 * NCTX), 2 * NCTX), :] = pre3[pl.ds(ch, 2 * NCTX, stride=16), :].astype(jnp.bfloat16)
        return c

    lax.fori_loop(0, NDP, widen, 0)

    def prefix(r, c):
        u = use[r] > 0
        for h in range(2):
            ln = pl.ds(h * 128, 128)
            q = qt_ref[r, :, ln]
            head = lane_head(HD)
            s = jnp.zeros((2 * NCTX * NDP, 128), jnp.float32)
            for k in range(4):
                s = s + lax.dot_general(pre4[4 * h + k], jnp.where(head == k, q, jnp.zeros_like(q)),
                    (((1,), (0,)), ((), ())), preferred_element_type=jnp.float32)
            s = s * SCALE
            m = jnp.max(s, axis=0, keepdims=True)
            w = jnp.exp(s - m).astype(jnp.bfloat16)
            l = jnp.sum(w.astype(jnp.float32), axis=0, keepdims=True)
            o = values_half([pre4[8 + 4 * h + k] for k in range(4)], w)
            m = jnp.where(u, m, LOW)
            l = jnp.where(u, l, 0.0)
            o = jnp.where(u, o, 0.0)
            old = big[r, :, ln]
            new = jnp.maximum(old, m)
            a, b = jnp.exp(old - new), jnp.exp(m - new)
            big[r, :, ln] = new
            tot[r, :, ln] = a * tot[r, :, ln] + b * l
            acc[r, :, ln] = a * acc[r, :, ln] + b * o
        return c

    lax.fori_loop(0, 16, prefix, 0)

    def merge(i, d):
        r0, r1 = req[2 * d], req[2 * d + 1]

        def one(r, c):
            l0 = jnp.where(r0 == r, recvl[i, 0:1, :], LOW)
            l1 = jnp.where(r1 == r, recvl[i, 1:2, :], LOW)
            old = big[r]
            new = jnp.maximum(old, jnp.maximum(l0, l1))
            a, b0, b1 = jnp.exp(old - new), jnp.exp(l0 - new), jnp.exp(l1 - new)
            big[r] = new
            tot[r] = a * tot[r] + b0 + b1
            acc[r] = a * acc[r] + b0 * recvp[i, 0].astype(jnp.float32) + b1 * recvp[i, 1].astype(jnp.float32)
            return c

        lax.fori_loop(0, 16, one, 0)

    merge(0, me)

    def take(i, c):
        l_copy(i).wait()
        p_copy(i).wait()
        merge(i, ahead(i))
        return c

    lax.fori_loop(1, NCTX, take, 0)

    def finish(r, c):
        out_ref[r] = (acc[r] * (1.0 / tot[r])).astype(jnp.bfloat16)
        return c

    lax.fori_loop(0, 16, finish, 0)


def body(queries, new_kv, kv_pages, page_owner, page_request, page_fill, prefix_kv, prefix_use):
    pages_dev, page_len, channels = kv_pages.shape
    request_count, step_count, query_width = queries.shape
    slots = 2 * NCTX
    owners = page_owner[:, 0]
    owner_hot = (owners[:, None] == jnp.arange(NCTX, dtype=jnp.int32)[None, :]).astype(jnp.int32)
    earlier = jnp.cumsum(owner_hot, axis=0) - owner_hot
    position = jnp.sum(earlier * owner_hot, axis=1)
    slot_of_page = owners * 2 + position
    matches = (slot_of_page[None, :] == jnp.arange(slots, dtype=jnp.int32)[:, None]).astype(jnp.int32)
    present = jnp.sum(matches, axis=1)
    page_of = jnp.sum(matches * jnp.arange(pages_dev, dtype=jnp.int32)[None, :], axis=1)
    send_request = jnp.where(present > 0, jnp.sum(matches * page_request[None, :], axis=1), -1)
    fill_of = jnp.maximum(jnp.sum(matches * page_fill[None, :], axis=1), 1)
    req = lax.all_to_all(send_request.reshape(NCTX, 2), "ctx", split_axis=0, concat_axis=0, tiled=True).reshape(slots)

    qt = queries.reshape(request_count, step_count, KVH * G, HD).transpose(0, 3, 2, 1).reshape(request_count, HD, 256)
    fresh = jnp.pad(new_kv, ((0, 0), (0, 12), (0, 0)))
    prefix = prefix_kv.reshape(32, 128)

    smem = pl.BlockSpec(memory_space=pltpu.SMEM)
    vmem = pl.BlockSpec(memory_space=pltpu.VMEM)
    dma = pltpu.SemaphoreType.DMA
    out = pl.pallas_call(
        kernel,
        out_shape=jax.ShapeDtypeStruct((request_count, HD, 256), jnp.bfloat16),
        in_specs=[smem] * 4 + [vmem] * 4,
        out_specs=vmem,
        scratch_shapes=[
            pltpu.VMEM((NCTX, 2, HD, 256), jnp.bfloat16),
            pltpu.VMEM((NCTX, 2, HD, 256), jnp.bfloat16),
            pltpu.VMEM((NCTX, 2, HD, 256), jnp.bfloat16),
            pltpu.VMEM((NCTX, 2, HD, 256), jnp.bfloat16),
            pltpu.VMEM((NCTX, 2, 256), jnp.float32),
            pltpu.VMEM((NCTX, 2, 256), jnp.float32),
            pltpu.VMEM((16, HD, 256), jnp.float32),
            pltpu.VMEM((16, 1, 256), jnp.float32),
            pltpu.VMEM((16, 1, 256), jnp.float32),
            pltpu.VMEM((NCTX, 32, 128), jnp.bfloat16),
            pltpu.VMEM((NDP, NCTX, 32, 128), jnp.bfloat16),
            pltpu.VMEM((NCTX * 32, 128), jnp.float32),
            pltpu.VMEM((16, 2 * NCTX * NDP, 128), jnp.bfloat16),
            dma((NCTX,)), dma((NCTX,)), dma((NCTX,)), dma((NCTX,)), dma((NCTX,)), dma((NCTX,)),
            dma((NCTX,)), dma((NCTX,)), dma((NDP,)), dma((NDP,)), dma,
        ],
        compiler_params=pltpu.CompilerParams(
            collective_id=0, has_side_effects=True, vmem_limit_bytes=60 * 2**20
        ),
    )(req, page_of, fill_of, prefix_use, qt, kv_pages, fresh, prefix)
    out = out.reshape(request_count, HD, KVH * G, step_count).transpose(0, 3, 2, 1)
    return out.reshape(request_count, step_count, query_width)


def solution(mesh):
    placed = (
        P(("ctx", "dp"), None, None),
        P(("ctx", "dp"), None, None),
        P(("ctx", "dp"), None, None),
        P(("ctx", "dp"), None),
        P(("ctx", "dp")),
        P(("ctx", "dp")),
        P(("ctx", "dp"), None),
        P(("ctx", "dp")),
    )
    return jax.shard_map(
        body, mesh=mesh, in_specs=placed, out_specs=P(("ctx", "dp"), None, None), check_vma=False
    )
```

time: 562 us -> 250 us (0.44)
  the two profiles are of different devices: /device:TPU:185 before, /device:TPU:32 now
where the time goes in v1:
time: 250 us
  Pallas kernels  220 us (88%)
  local copies, waits for them, and re-layouts  13.4 us (5%)
  starting transfers between devices  11.4 us (5%)
  other arithmetic  4.84 us (2%)
    pallas_call x1, Pallas kernels, body(): pl.pallas_call(kernel, out_shape=jax.ShapeDtypeStruct((request_count, HD,...  220 us
    all_to_all x1, starting transfers between devices, body(): lax.all_to_all(send_request.reshape(NCTX, 2), 'ctx', split_axis=0, concat...  11.4 us
  transfers between devices with their start and end apart: 1, of which 1 were waited for; matrix products, arithmetic and copies ran while one was open for 3% of the time, Pallas kernels for 0%

profile of v1, /device:TPU:32, one launch (start us, length us, event | category | flops | bytes accessed | tf_op | source)
XLA Modules:
  0.0 250.2 jit_solution(10098769868839667466)
XLA Ops:
  0.0 0.7 fusion
  0.7 0.1 reduce_window_sum.11
  0.8 0.8 select_reduce_fusion.3
  1.6 0.7 multiply_add_fusion
  2.3 1.3 select_reduce_fusion
  3.6 0.7 select_n.16
  4.3 11.4 %all-to-all-start = ((s32[32,1,2]{2,1,0:T(1,128)}), s32[32,1,2]{2,1,0:T(1,128)S(1)}, u32[]{:S(2)}, u32[]{:S(2)}) async-start(s32[32,1,2]{2,1,0:T(1,128)} %bitcast.1), calls=%async_computation | async-start | bytes 32768 | tf_op jit(solution)/shard_map/all_to_all | solution.py:282
  15.7 0.5 broadcast_maximum_fusion.fill_of
  16.2 1.3 reshape.61.prefix_ref
  17.5 2.1 reshape.64
  19.6 0.7 copy.28
  20.3 1.6 copy.29.qt_ref
  21.9 2.1 pad.4.fresh_ref
  24.0 0.3 all-to-all-done
  24.3 0.6 broadcast.45
  24.9 0.7 reduce.3
  25.6 0.6 reshape.58.req
  26.2 220.2 %shard_map.82 = bf16[16,128,256]{2,1,0:T(8,128)(2,1)} custom-call(s32[64]{0:T(128)} %reshape.58.req, s32[64]{0:T(128)} %get-tuple-element.6.page_of, s32[64]{0:T(128)} %broadcast_maximum_fusion.fill_of, s32[16]{0:T(128)} %use.1, bf16[16,128,256]{2,1,0:T(8,128)(2,1)} %copy.29.qt_ref, bf16[32,64,2048]{2,1,0:T(8,128)(2,1)} %pages_ref.1, ...), custom_call_target="tpu_custom_call" | custom-call | tf_op jit(solution)/shard_map/pallas_call | solution.py:291
  246.4 1.9 copy.30
  248.4 0.7 copy.35
  249.0 1.1 reshape.65
  (1 shorter events, 0.0 us)
Async XLA Ops:
  4.3 20.0 %all-to-all-start = ((s32[32,1,2]{2,1,0:T(1,128)}), s32[32,1,2]{2,1,0:T(1,128)S(1)}, u32[]{:S(2)}, u32[]{:S(2)}) async-start(s32[32,1,2]{2,1,0:T(1,128)} %bitcast.1), calls=%async_computation | async-start | bytes 32768 | tf_op jit(solution)/shard_map/all_to_all | solution.py:282

commit v2 on v1

v2 whole, which is shorter than its diff:
```python
import functools
import math

import jax
import jax.numpy as jnp
from jax import lax
from jax.experimental import pallas as pl
from jax.experimental.pallas import tpu as pltpu
from jax.sharding import PartitionSpec as P

KVH = 8
HD = 128
G = 8
LOW = -1e30
NY, NZ = 4, 8
NCTX = NY * NZ
NDP = 8
EARLY = 32
RELAY = 12
TAKEN = 20
MESH = pl.DeviceIdType.MESH
SCALE = 1.0 / math.sqrt(HD)


def meta_kernel(owner, request, fill, table, own, level, mine, tally, sa, ra, sb, rb):
    me = lax.axis_index("ctx")
    col = lax.axis_index("dp")
    y, z = me // NZ, me % NZ

    def ahead(i):
        return ((y + i // NZ) % NY) * NZ + (z + i % NZ) % NZ

    barrier = pltpu.get_barrier_semaphore()
    for i in range(1, NCTX):
        pl.semaphore_signal(barrier, inc=1, device_id={"ctx": ahead(i)}, device_id_type=MESH)
    for i in range(1, NDP):
        pl.semaphore_signal(barrier, inc=1, device_id={"dp": (col + i) % NDP}, device_id_type=MESH)

    lane = lax.broadcasted_iota(jnp.int32, (8, 128), 1)
    count = jnp.zeros((8, 128), jnp.int32)
    r0 = jnp.full((8, 128), -1, jnp.int32)
    r1, p0, p1, f0, f1 = r0, count, count, count + 1, count + 1
    for p in range(owner.shape[0]):
        hit = lane == owner[p, 0]
        first, second = hit & (count == 0), hit & (count == 1)
        r0, r1 = jnp.where(first, request[p], r0), jnp.where(second, request[p], r1)
        p0, p1 = jnp.where(first, p, p0), jnp.where(second, p, p1)
        f0, f1 = jnp.where(first, fill[p], f0), jnp.where(second, fill[p], f1)
        count = count + hit.astype(jnp.int32)
    own[0:1, :] = p0[0:1]
    own[1:2, :] = p1[0:1]
    own[2:3, :] = f0[0:1]
    own[3:4, :] = f1[0:1]
    extra = jnp.where(count == 2, 1, 0)
    whole = extra
    for k in range(1, NY):
        whole = whole + pltpu.roll(extra, k * NZ, 1)
    most = jnp.max(whole, axis=1, keepdims=True)
    tally[0] = jnp.broadcast_to(most, (8, 128))

    pl.semaphore_wait(barrier, NCTX + NDP - 2)

    def tally_copy(i):
        return pltpu.make_async_remote_copy(
            src_ref=tally.at[0], dst_ref=tally.at[i], send_sem=sa.at[i], recv_sem=ra.at[i],
            device_id={"dp": (col + i) % NDP}, device_id_type=MESH)

    for i in range(1, NDP):
        tally_copy(i).start()
    for i in range(1, NDP):
        tally_copy(i).wait()
    most = tally[0]
    for i in range(1, NDP):
        most = jnp.maximum(most, tally[i])
    row = jnp.where(lane < NCTX, r0, jnp.where(lane < 2 * NCTX, pltpu.roll(r1, NCTX, 1), most))
    mine[0] = row[0:1]
    table[pl.ds(me, 1)] = row[0:1].reshape(1, 1, 128)

    def row_copy(i):
        return pltpu.make_async_remote_copy(
            src_ref=mine.at[0], dst_ref=table.at[me], send_sem=sb.at[i], recv_sem=rb.at[i],
            device_id={"ctx": ahead(i)}, device_id_type=MESH)

    for i in range(1, NCTX):
        row_copy(i).start()
    for i in range(1, NCTX):
        row_copy(i).wait()
    far = table[0]
    for h in range(1, NCTX):
        far = jnp.maximum(far, table[h])
    need = jnp.max(jnp.where(lax.broadcasted_iota(jnp.int32, (1, 128), 1) >= 2 * NCTX, far, 0), axis=1, keepdims=True)
    level[...] = jnp.broadcast_to(jnp.where(need <= 1, 0, jnp.where(need <= 2, 1, 2)), (1, 128))


def lane_head(rows):
    return lax.broadcasted_iota(jnp.int32, (rows, 128), 1) // 32


def spread(block, rows):
    head = lane_head(rows)
    zero = jnp.zeros_like(block)
    return jnp.concatenate([jnp.where(head == k, block, zero) for k in range(4)], axis=0)


def values_half(values, w):
    stacked = jnp.concatenate(values, axis=0)
    return lax.dot_general(
        stacked, spread(w, w.shape[0]), (((0,), (0,)), ((), ())), preferred_element_type=jnp.float32
    )


def group_half(keys, values, qt, visible):
    s = lax.dot_general(
        keys, spread(qt, HD), (((1,), (0,)), ((), ())), preferred_element_type=jnp.float32
    ) * SCALE
    s = jnp.where(visible, s, LOW)
    m = jnp.max(s, axis=0, keepdims=True)
    w = jnp.where(visible, jnp.exp(s - m), 0.0).astype(jnp.bfloat16)
    l = jnp.sum(w.astype(jnp.float32), axis=0, keepdims=True)
    return m, l, values_half(values, w)


def kernel(
    cap, table, own, use,
    qt_ref, pages_hbm, fresh_ref, prefix_ref,
    out_ref,
    pages_ref, sq, rq, sp, rp, sl, rl,
    sq2, rq2, spk, rpk, sp2, rp2, sl2, rl2, su, ru, sul, rul,
    acc, big, tot, pre0, pre1, pre2, pre3, pre4,
    sq_s, rq_s, sp_s, rp_s, sl_s, rl_s,
    sq2_s, rq2_s, spk_s, rpk_s, sp2_s, rp2_s, sl2_s, rl2_s, su_s, ru_s, sul_s, rul_s,
    a_s, a_r, b_s, b_r, c_s, c_r, page_s,
):
    me = lax.axis_index("ctx")
    col = lax.axis_index("dp")
    y, z = me // NZ, me % NZ

    page_load = pltpu.make_async_copy(pages_hbm, pages_ref, page_s)
    page_load.start()

    def at(a, b):
        return (a % NY) * NZ + b % NZ

    def ahead(i):
        return at(y + i // NZ, z + i % NZ)

    def behind(i):
        return at(y + NY - i // NZ, z + NZ - i % NZ)

    def remote(src, dst, send, recv, ctx):
        return pltpu.make_async_remote_copy(
            src_ref=src, dst_ref=dst, send_sem=send, recv_sem=recv,
            device_id={"ctx": ctx}, device_id_type=MESH)

    def loop(lo, hi, f):
        def step(i, c):
            f(i)
            return c

        lax.fori_loop(lo, hi, step, 0)

    barrier = pltpu.get_barrier_semaphore()
    loop(1, NCTX, lambda i: pl.semaphore_signal(barrier, inc=1, device_id={"ctx": ahead(i)}, device_id_type=MESH))
    loop(1, NDP, lambda i: pl.semaphore_signal(barrier, inc=1, device_id={"dp": (col + i) % NDP}, device_id_type=MESH))
    pl.semaphore_wait(barrier, NCTX + NDP - 2)

    def pre_z(i):
        return remote(prefix_ref, pre0.at[i], a_s.at[i], a_r.at[i], at(y, z + i))

    def pre_y(i):
        return remote(pre0, pre1.at[i], b_s.at[i], b_r.at[i], at(y + i, z))

    def pre_dp(i):
        return pltpu.make_async_remote_copy(
            src_ref=pre1, dst_ref=pre2.at[i], send_sem=c_s.at[i], recv_sem=c_r.at[i],
            device_id={"dp": (col + i) % NDP}, device_id_type=MESH)

    loop(1, NZ, lambda i: pre_z(i).start())
    pre0[0] = prefix_ref[...]

    def q2_copy(i):
        return remote(sq2.at[i], rq2.at[i], sq2_s.at[i], rq2_s.at[i], at(y + i, z))

    def wanted(h, second):
        return qt_ref[jnp.maximum(table[h, 0, second * NCTX + me], 0)]

    def relay_queries(i):
        def one(zh):
            sq2[i, zh] = wanted(at(y + i, zh), 1)

        loop(0, NZ, one)
        q2_copy(i).start()

    def q_copy(i):
        return remote(sq.at[i], rq.at[i], sq_s.at[i], rq_s.at[i], ahead(i))

    def send_queries(i):
        sq[i] = wanted(ahead(i), 0)
        q_copy(i).start()

    loop(1, NY, relay_queries)
    loop(1, NCTX, send_queries)
    rq[0] = wanted(me, 0)

    def own_relay(zh):
        rq2[0, zh] = wanted(at(y, zh), 1)

    loop(0, NZ, own_relay)

    loop(1, NZ, lambda i: pre_z(i).wait())
    loop(1, NY, lambda i: pre_y(i).start())
    pre1[0] = pre0[...]

    t = lax.broadcasted_iota(jnp.int32, (16, 128), 0)
    causal = t <= lax.broadcasted_iota(jnp.int32, (16, 128), 1) % 4

    def fresh(r):
        for h in range(2):
            ln = pl.ds(h * 128, 128)
            keys = fresh_ref[r, :, pl.ds(h * 512, 512)]
            values = [fresh_ref[r, :, pl.ds(1024 + (4 * h + k) * 128, 128)] for k in range(4)]
            m, l, o = group_half(keys, values, qt_ref[r, :, ln], causal)
            big[r, :, ln] = m
            tot[r, :, ln] = l
            acc[r, :, ln] = o

    loop(0, 16, fresh)

    loop(1, NY, lambda i: pre_y(i).wait())
    loop(1, NDP, lambda i: pre_dp(i).start())
    pre2[0] = pre1[...]

    page_load.wait()

    def attend(q, p, f, put_o, put_l):
        visible = lax.broadcasted_iota(jnp.int32, (64, 128), 0) < f
        for h in range(2):
            ln = pl.ds(h * 128, 128)
            keys = pages_ref[p, :, pl.ds(h * 512, 512)]
            values = [pages_ref[p, :, pl.ds(1024 + (4 * h + k) * 128, 128)] for k in range(4)]
            m, l, out = group_half(keys, values, q[:, ln], visible)
            put_o[:, ln] = (out * (1.0 / l)).astype(jnp.bfloat16)
            put_l[:, ln] = m + jnp.log(l)

    def p_copy(i):
        return remote(sp.at[i], rp.at[i], sp_s.at[i], rp_s.at[i], behind(i))

    def l_copy(i):
        return remote(sl.at[i], rl.at[i], sl_s.at[i], rl_s.at[i], behind(i))

    def answer(i):
        q_copy(i).wait()
        o = behind(i)
        attend(rq.at[i], own[0, o], own[2, o], sp.at[i], sl.at[i])
        l_copy(i).start()
        p_copy(i).start()

    attend(rq.at[0], own[0, me], own[2, me], rp.at[0], rl.at[0])

    def in_use(h, plane):
        return [(table[h, 0, NCTX + k * NZ + plane] >= 0).astype(jnp.int32) for k in range(NY)]

    def nth(flags, j):
        place, seen = 0, 0
        for k in range(NY):
            place = jnp.where((flags[k] == 1) & (seen == j), k, place)
            seen = seen + flags[k]
        return place

    def pack_copy(d):
        return remote(spk.at[d], rpk.at[d], spk_s.at[d], rpk_s.at[d], at(y, z + d))

    def pack(d, dst):
        zh = (z + d) % NZ
        flags = in_use(at(y, zh), z)
        for j in range(cap):
            dst[d, j] = rq2[(y + NY - nth(flags, j)) % NY, zh]

    def pack_send(d):
        pack(d, spk)
        pack_copy(d).start()

    def p2_copy(d):
        return remote(sp2.at[d], rp2.at[d], sp2_s.at[d], rp2_s.at[d], at(y, z + NZ - d))

    def l2_copy(d):
        return remote(sl2.at[d], rl2.at[d], sl2_s.at[d], rl2_s.at[d], at(y, z + NZ - d))

    def attend2(d, dst_o, dst_l):
        plane = (z + NZ - d) % NZ
        flags = in_use(me, plane)
        for j in range(cap):
            o = nth(flags, j) * NZ + plane
            attend(rpk.at[d, j], own[1, o], own[3, o], dst_o.at[d, j], dst_l.at[d, j])

    def answer2(d):
        pack_copy(d).wait()
        attend2(d, sp2, sl2)
        l2_copy(d).start()
        p2_copy(d).start()

    def u_copy(i, zh):
        return remote(su.at[i, zh], ru.at[i, zh], su_s.at[i, zh], ru_s.at[i, zh], at(y + i, z))

    def ul_copy(i, zh):
        return remote(sul.at[i, zh], rul.at[i, zh], sul_s.at[i, zh], rul_s.at[i, zh], at(y + i, z))

    def hand_on(d):
        zh = (z + d) % NZ
        flags = in_use(at(y, zh), z)
        for i in range(NY):
            k = (y + i) % NY
            before = 0
            for k2 in range(NY):
                before = before + jnp.where(k2 < k, flags[k2], 0)
            o, l = rp2[d, 0], rl2[d, 0]
            for j in range(1, cap):
                o, l = jnp.where(before >= j, rp2[d, j], o), jnp.where(before >= j, rl2[d, j], l)
            if i == 0:
                ru[0, zh] = o
                rul[0, zh] = l
            else:
                su[i, zh] = o
                sul[i, zh] = l
                ul_copy(i, zh).start()
                u_copy(i, zh).start()

    loop(1, RELAY, answer)
    loop(1, NY, lambda i: q2_copy(i).wait())
    loop(1, NZ, pack_send)
    pack(0, rpk)
    attend2(0, rp2, rl2)
    loop(RELAY, EARLY, answer)
    loop(1, NZ, answer2)
    loop(EARLY, NCTX, answer)

    loop(1, NDP, lambda i: pre_dp(i).wait())

    def widen(i):
        pre3[...] = pre2[i].astype(jnp.float32).reshape(NCTX * 32, 128)
        for ch in range(16):
            pre4[ch, pl.ds(pl.multiple_of(i * 2 * NCTX, 2 * NCTX), 2 * NCTX), :] = pre3[
                pl.ds(ch, 2 * NCTX, stride=16), :].astype(jnp.bfloat16)

    loop(0, NDP, widen)

    def prefix(r):
        u = use[r] > 0
        for h in range(2):
            ln = pl.ds(h * 128, 128)
            q = qt_ref[r, :, ln]
            head = lane_head(HD)
            s = jnp.zeros((2 * NCTX * NDP, 128), jnp.float32)
            for k in range(4):
                s = s + lax.dot_general(
                    pre4[4 * h + k], jnp.where(head == k, q, jnp.zeros_like(q)),
                    (((1,), (0,)), ((), ())), preferred_element_type=jnp.float32)
            s = s * SCALE
            m = jnp.max(s, axis=0, keepdims=True)
            w = jnp.exp(s - m).astype(jnp.bfloat16)
            l = jnp.sum(w.astype(jnp.float32), axis=0, keepdims=True)
            o = values_half([pre4[8 + 4 * h + k] for k in range(4)], w)
            m = jnp.where(u, m, LOW)
            l = jnp.where(u, l, 0.0)
            o = jnp.where(u, o, 0.0)
            old = big[r, :, ln]
            new = jnp.maximum(old, m)
            a, b = jnp.exp(old - new), jnp.exp(m - new)
            big[r, :, ln] = new
            tot[r, :, ln] = a * tot[r, :, ln] + b * l
            acc[r, :, ln] = a * acc[r, :, ln] + b * o

    loop(0, 16, prefix)

    def merge(items):
        def one(r):
            ls = [jnp.where(q == r, l[...], LOW) for q, l, _ in items]
            old = big[r]
            new = functools.reduce(jnp.maximum, ls, old)
            a = jnp.exp(old - new)
            bs = [jnp.exp(l - new) for l in ls]
            big[r] = new
            tot[r] = functools.reduce(lambda x, b: x + b, bs, a * tot[r])
            more = a * acc[r]
            for b, (_, _, o) in zip(bs, items):
                more = more + b * o[...].astype(jnp.float32)
            acc[r] = more

        loop(0, 16, one)

    def take(k):
        def arrive(i):
            l_copy(i).wait()
            p_copy(i).wait()

        loop(4 * k, 4 * k + 4, arrive)
        merge([(table[ahead(4 * k + n), 0, me], rl.at[4 * k + n], rp.at[4 * k + n]) for n in range(4)])

    def arrive(i):
        l_copy(i).wait()
        p_copy(i).wait()

    loop(1, 4, arrive)
    merge([(table[ahead(n), 0, me], rl.at[n], rp.at[n]) for n in range(4)])
    loop(1, TAKEN // 4, take)

    def relay_back(d):
        l2_copy(d).wait()
        p2_copy(d).wait()
        hand_on(d)

    hand_on(0)
    loop(1, NZ, relay_back)
    loop(TAKEN // 4, NCTX // 4, take)

    def merge_second(i, zh):
        n = min(4, NZ)
        hs = [zh + j for j in range(n)]
        merge([(table[at(y + NY - i, h), 0, NCTX + me], rul.at[i, h], ru.at[i, h]) for h in hs])

    def take_second(i):
        def arrive2(zh):
            ul_copy(i, zh).wait()
            u_copy(i, zh).wait()

        loop(0, NZ, arrive2)
        loop(0, max(1, NZ // 4), lambda k: merge_second(i, 4 * k))

    loop(0, max(1, NZ // 4), lambda k: merge_second(0, 4 * k))
    loop(1, NY, take_second)

    def finish(r):
        out_ref[r] = (acc[r] * (1.0 / tot[r])).astype(jnp.bfloat16)

    loop(0, 16, finish)


def attend_all(cap, table, own, use, qt, pages, fresh, prefix):
    smem = pl.BlockSpec(memory_space=pltpu.SMEM)
    vmem = pl.BlockSpec(memory_space=pltpu.VMEM)
    dma = pltpu.SemaphoreType.DMA

    def rows(*lead):
        return pltpu.VMEM(lead + (HD, 256), jnp.bfloat16)

    def stats(*lead):
        return pltpu.VMEM(lead + (1, 256), jnp.float32)

    return pl.pallas_call(
        functools.partial(kernel, cap),
        out_shape=jax.ShapeDtypeStruct(qt.shape, jnp.bfloat16),
        in_specs=[smem] * 3 + [vmem, pl.BlockSpec(memory_space=pl.ANY), vmem, vmem],
        out_specs=vmem,
        scratch_shapes=[
            pltpu.VMEM(pages.shape, jnp.bfloat16),
            rows(NCTX), rows(NCTX), rows(NCTX), rows(NCTX), stats(NCTX), stats(NCTX),
            rows(NY, NZ), rows(NY, NZ), rows(NZ, cap), rows(NZ, cap), rows(NZ, cap), rows(NZ, cap),
            stats(NZ, cap), stats(NZ, cap), rows(NY, NZ), rows(NY, NZ), stats(NY, NZ), stats(NY, NZ),
            pltpu.VMEM((16, HD, 256), jnp.float32), stats(16), stats(16),
            pltpu.VMEM((NZ, 32, 128), jnp.bfloat16),
            pltpu.VMEM((NY, NZ, 32, 128), jnp.bfloat16),
            pltpu.VMEM((NDP, NY, NZ, 32, 128), jnp.bfloat16),
            pltpu.VMEM((NCTX * 32, 128), jnp.float32),
            pltpu.VMEM((16, 2 * NCTX * NDP, 128), jnp.bfloat16),
            dma((NCTX,)), dma((NCTX,)), dma((NCTX,)), dma((NCTX,)), dma((NCTX,)), dma((NCTX,)),
            dma((NY,)), dma((NY,)), dma((NZ,)), dma((NZ,)), dma((NZ,)), dma((NZ,)), dma((NZ,)), dma((NZ,)),
            dma((NY, NZ)), dma((NY, NZ)), dma((NY, NZ)), dma((NY, NZ)),
            dma((NZ,)), dma((NZ,)), dma((NY,)), dma((NY,)), dma((NDP,)), dma((NDP,)), dma,
        ],
        compiler_params=pltpu.CompilerParams(
            collective_id=cap, has_side_effects=True, vmem_limit_bytes=60 * 2**20
        ),
        name="attend%d" % cap,
    )(table, own, use, qt, pages, fresh, prefix)


def body(queries, new_kv, kv_pages, page_owner, page_request, page_fill, prefix_kv, prefix_use):
    request_count, step_count, query_width = queries.shape
    smem = pl.BlockSpec(memory_space=pltpu.SMEM)
    vmem = pl.BlockSpec(memory_space=pltpu.VMEM)
    dma = pltpu.SemaphoreType.DMA
    table, own, level = pl.pallas_call(
        meta_kernel,
        out_shape=[
            jax.ShapeDtypeStruct((NCTX, 1, 128), jnp.int32),
            jax.ShapeDtypeStruct((4, 128), jnp.int32),
            jax.ShapeDtypeStruct((1, 128), jnp.int32),
        ],
        in_specs=[smem] * 3,
        out_specs=[vmem] * 3,
        scratch_shapes=[
            pltpu.VMEM((1, 1, 128), jnp.int32),
            pltpu.VMEM((NDP, 8, 128), jnp.int32),
            dma((NDP,)), dma((NDP,)), dma((NCTX,)), dma((NCTX,)),
        ],
        compiler_params=pltpu.CompilerParams(collective_id=0, has_side_effects=True),
        name="meta",
    )(page_owner, page_request, page_fill)

    qt = queries.reshape(request_count, step_count, KVH * G, HD).transpose(0, 3, 2, 1).reshape(request_count, HD, 256)
    fresh = jnp.pad(new_kv, ((0, 0), (0, 12), (0, 0)))
    prefix = prefix_kv.reshape(32, 128)
    out = lax.switch(
        level[0, 0],
        [functools.partial(attend_all, cap) for cap in (1, 2, 4)],
        table, own, prefix_use, qt, kv_pages, fresh, prefix,
    )
    out = out.reshape(request_count, HD, KVH * G, step_count).transpose(0, 3, 2, 1)
    return out.reshape(request_count, step_count, query_width)


def solution(mesh):
    placed = (
        P(("ctx", "dp"), None, None),
        P(("ctx", "dp"), None, None),
        P(("ctx", "dp"), None, None),
        P(("ctx", "dp"), None),
        P(("ctx", "dp")),
        P(("ctx", "dp")),
        P(("ctx", "dp"), None),
        P(("ctx", "dp")),
    )
    return jax.shard_map(
        body, mesh=mesh, in_specs=placed, out_specs=P(("ctx", "dp"), None, None), check_vma=False
    )
```

time: 250 us -> 206 us (0.82)
  Pallas kernels: 220 us -> 194 us
  starting transfers between devices: 11.4 us -> 0 us
  other arithmetic: 4.84 us -> 0 us
  local copies, waits for them, and re-layouts: 13.4 us -> 10.4 us
    pallas_call x1 -> x2, Pallas kernels: 220 us -> 194 us  [the longest x1 174 us: attend_all(): pl.pallas_call(functools.partial(kernel, cap), out_shape=jax.ShapeDtypeSt...]
    all_to_all x1 -> x0, starting transfers between devices: 11.4 us -> none  [body(): lax.all_to_all(send_request.reshape(NCTX, 2), 'ctx', split_axis=0, concat...]
  transfers between devices with their start and end apart: 1 -> 0, of which waited for: 1 -> 0; matrix products, arithmetic and copies ran while one was open for 3% -> 0% of each run, Pallas kernels for 0% -> 0%
where the time goes in v2:
time: 206 us
  Pallas kernels  194 us (94%)
  local copies, waits for them, and re-layouts  10.4 us (5%)
    pallas_call x1, Pallas kernels, attend_all(): pl.pallas_call(functools.partial(kernel, cap), out_shape=jax.ShapeDtypeSt...  174 us
    pallas_call x1, Pallas kernels, body(): pl.pallas_call(meta_kernel, out_shape=[jax.ShapeDtypeStruct((NCTX, 1, 128...  20.2 us

profile of v2, /device:TPU:32, one launch (start us, length us, event | category | flops | bytes accessed | tf_op | source)
XLA Modules:
  0.0 205.9 jit_solution(11047555744628518744)
XLA Ops:
  0.0 0.7 reshape.20
  0.7 1.3 copy.17.owner
  2.0 20.2 %meta.1 = (s32[32,1,128]{2,1,0:T(1,128)S(1)}, s32[4,128]{1,0:T(4,128)S(1)}, s32[1,128]{1,0:T(1,128)}) custom-call(s32[32,1]{1,0:T(8,128)} %copy.17.owner, s32[32]{0:T(128)} %request.1, s32[32]{0:T(128)} %fill.1), custom_call_target="tpu_custom_call" | custom-call | tf_op jit(solution)/shard_map/meta/pallas_call | solution.py:482
  22.9 2.1 %reshape.23 = bf16[16,4,64,128]{3,2,1,0:T(8,128)(2,1)S(1)} reshape(bf16[16,4,8192]{2,1,0:T(4,128)(2,1)} %param.11) | data formatting | bytes 2097152 | tf_op jit(solution)/shard_map/reshape | solution.py:500
  25.0 0.7 copy.19
  25.7 1.1 pad.4
  26.8 176.1 %conditional.1 = (bf16[16,128,256]{2,1,0:T(8,128)(2,1)S(1)}) conditional(s32[]{:T(128)} %bitcast, (s32[32,1,128]{2,1,0:T(1,128)S(1)}, s32[4,128]{1,0:T(4,128)S(1)}, s32[16]{0:T(128)}, bf16[16,128,256]{1,0,2:T(8,128)(2,1)S(1)}, bf16[32,64,2048]{2,1,0:T(8,128)(2,1)}, /*index=5*/bf16[16,16,2048]{2,1,0:T(8,128)(2,1)S(1)}, ...), branch_computations={%region_0.1_spmd, %region_1.2_spmd, %region_2.3_spmd} | conditional | bytes 2097160 | solution.py:503
  27.0 1.6 copy.21.qt_ref
  28.6 174.1 %attend2.1 = bf16[16,128,256]{2,1,0:T(8,128)(2,1)S(1)} custom-call(s32[32,1,128]{2,1,0:T(1,128)S(1)} %get-tuple-element.58.table, s32[4,128]{1,0:T(4,128)S(1)} %get-tuple-element.59.own, s32[16]{0:T(128)} %get-tuple-element.60.use, bf16[16,128,256]{2,1,0:T(8,128)(2,1)} %copy.21.qt_ref, bf16[32,64,2048]{2,1,0:T(8,128)(2,1)} %get-tuple-element.62.pages_hbm, ...), custom_call_target="tpu_custom_call" | custom-call | tf_op jit(solution)/shard_map/cond/branch_1_fun/attend2/pallas_call | solution.py:449
  203.0 1.1 copy.23
  204.1 0.7 copy.28
  204.8 1.1 reshape.24

commit v3 on v2

--- a/solution.py
+++ b/solution.py
@@ -22,69 +22,107 @@
 SCALE = 1.0 / math.sqrt(HD)
 
 
-def meta_kernel(owner, request, fill, table, own, level, mine, tally, sa, ra, sb, rb):
+def meta_kernel(
+    owner, request, fill, q_ref, prefix_ref,
+    table, own, level, qt_ref, rows_ref,
+    tally, wide, sa, ra, sb, rb, sc, rc,
+):
     me = lax.axis_index("ctx")
     col = lax.axis_index("dp")
     y, z = me // NZ, me % NZ
 
-    def ahead(i):
-        return ((y + i // NZ) % NY) * NZ + (z + i % NZ) % NZ
+    def near(i):
+        return y * NZ + (z + i) % NZ
+
+    def across(i):
+        return ((y + i) % NY) * NZ + z
 
     barrier = pltpu.get_barrier_semaphore()
-    for i in range(1, NCTX):
-        pl.semaphore_signal(barrier, inc=1, device_id={"ctx": ahead(i)}, device_id_type=MESH)
     for i in range(1, NDP):
         pl.semaphore_signal(barrier, inc=1, device_id={"dp": (col + i) % NDP}, device_id_type=MESH)
+    for i in range(1, NZ):
+        pl.semaphore_signal(barrier, inc=1, device_id={"ctx": near(i)}, device_id_type=MESH)
+    for i in range(1, NY):
+        pl.semaphore_signal(barrier, inc=1, device_id={"ctx": across(i)}, device_id_type=MESH)
 
     lane = lax.broadcasted_iota(jnp.int32, (8, 128), 1)
     count = jnp.zeros((8, 128), jnp.int32)
     r0 = jnp.full((8, 128), -1, jnp.int32)
     r1, p0, p1, f0, f1 = r0, count, count, count + 1, count + 1
     for p in range(owner.shape[0]):
-        hit = lane == owner[p, 0]
+        hit = lane == owner[p]
         first, second = hit & (count == 0), hit & (count == 1)
         r0, r1 = jnp.where(first, request[p], r0), jnp.where(second, request[p], r1)
         p0, p1 = jnp.where(first, p, p0), jnp.where(second, p, p1)
         f0, f1 = jnp.where(first, fill[p], f0), jnp.where(second, fill[p], f1)
         count = count + hit.astype(jnp.int32)
+    extra = jnp.where(count == 2, 1, 0)
+    whole = extra
+    for k in range(1, NY):
+        whole = whole + pltpu.roll(extra, k * NZ, 1)
+    tally[0] = jnp.broadcast_to(jnp.max(whole, axis=1, keepdims=True), (8, 128))
+
+    pl.semaphore_wait(barrier, NDP + NZ + NY - 3)
+
+    def tally_copy(i):
+        return pltpu.make_async_remote_copy(
+            src_ref=tally.at[0], dst_ref=tally.at[i], send_sem=sa.at[i], recv_sem=ra.at[i],
+            device_id={"dp": (col + i) % NDP}, device_id_type=MESH)
+
+    for i in range(1, NDP):
+        tally_copy(i).start()
+
     own[0:1, :] = p0[0:1]
     own[1:2, :] = p1[0:1]
     own[2:3, :] = f0[0:1]
     own[3:4, :] = f1[0:1]
-    extra = jnp.where(count == 2, 1, 0)
-    whole = extra
-    for k in range(1, NY):
-        whole = whole + pltpu.roll(extra, k * NZ, 1)
-    most = jnp.max(whole, axis=1, keepdims=True)
-    tally[0] = jnp.broadcast_to(most, (8, 128))
-
-    pl.semaphore_wait(barrier, NCTX + NDP - 2)
-
-    def tally_copy(i):
-        return pltpu.make_async_remote_copy(
-            src_ref=tally.at[0], dst_ref=tally.at[i], send_sem=sa.at[i], recv_sem=ra.at[i],
-            device_id={"dp": (col + i) % NDP}, device_id_type=MESH)
-
-    for i in range(1, NDP):
-        tally_copy(i).start()
+
+    def turn(lo, hi):
+        def one(r, c):
+            for h in range(2):
+                x = q_ref[r, :, pl.ds(h * 4096, 4096)].astype(jnp.float32)
+                x = jnp.concatenate([x[:, k * 128:(k + 1) * 128] for k in range(32)], axis=0)
+                qt_ref[r, :, pl.ds(h * 128, 128)] = x.T.astype(jnp.bfloat16)
+            return c
+
+        lax.fori_loop(lo, hi, one, 0)
+
+    turn(0, 5)
     for i in range(1, NDP):
         tally_copy(i).wait()
     most = tally[0]
     for i in range(1, NDP):
         most = jnp.maximum(most, tally[i])
     row = jnp.where(lane < NCTX, r0, jnp.where(lane < 2 * NCTX, pltpu.roll(r1, NCTX, 1), most))
-    mine[0] = row[0:1]
     table[pl.ds(me, 1)] = row[0:1].reshape(1, 1, 128)
 
     def row_copy(i):
         return pltpu.make_async_remote_copy(
-            src_ref=mine.at[0], dst_ref=table.at[me], send_sem=sb.at[i], recv_sem=rb.at[i],
-            device_id={"ctx": ahead(i)}, device_id_type=MESH)
-
-    for i in range(1, NCTX):
+            src_ref=table.at[me], dst_ref=table.at[me], send_sem=sb.at[i], recv_sem=rb.at[i],
+            device_id={"ctx": near(i)}, device_id_type=MESH)
+
+    for i in range(1, NZ):
         row_copy(i).start()
-    for i in range(1, NCTX):
+    turn(5, 11)
+    x = prefix_ref[...].astype(jnp.float32)
+    for t in range(2):
+        for c in range(16):
+            wide[pl.ds(t * 16 + c, 1), :] = x[t:t + 1, c * 128:(c + 1) * 128]
+    rows_ref[...] = wide[...].astype(jnp.bfloat16)
+    for i in range(1, NZ):
         row_copy(i).wait()
+
+    def line_copy(i):
+        line = table.at[pl.ds(y * NZ, NZ)]
+        return pltpu.make_async_remote_copy(
+            src_ref=line, dst_ref=line, send_sem=sc.at[i], recv_sem=rc.at[i],
+            device_id={"ctx": across(i)}, device_id_type=MESH)
+
+    for i in range(1, NY):
+        line_copy(i).start()
+    turn(11, 16)
+    for i in range(1, NY):
+        line_copy(i).wait()
     far = table[0]
     for h in range(1, NCTX):
         far = jnp.maximum(far, table[h])
@@ -126,7 +164,7 @@
     out_ref,
     pages_ref, sq, rq, sp, rp, sl, rl,
     sq2, rq2, spk, rpk, sp2, rp2, sl2, rl2, su, ru, sul, rul,
-    acc, big, tot, pre0, pre1, pre2, pre3, pre4,
+    acc, big, tot, pre0, pre1, pre2, pre3, pre4, new16,
     sq_s, rq_s, sp_s, rp_s, sl_s, rl_s,
     sq2_s, rq2_s, spk_s, rpk_s, sp2_s, rp2_s, sl2_s, rl2_s, su_s, ru_s, sul_s, rul_s,
     a_s, a_r, b_s, b_r, c_s, c_r, page_s,
@@ -162,6 +200,18 @@
     barrier = pltpu.get_barrier_semaphore()
     loop(1, NCTX, lambda i: pl.semaphore_signal(barrier, inc=1, device_id={"ctx": ahead(i)}, device_id_type=MESH))
     loop(1, NDP, lambda i: pl.semaphore_signal(barrier, inc=1, device_id={"dp": (col + i) % NDP}, device_id_type=MESH))
+    def wanted(h, second):
+        return qt_ref[jnp.maximum(table[h, 0, second * NCTX + me], 0)]
+
+    def second_queries(k):
+        i, zh = k // NZ, k % NZ
+        sq2[i, zh] = wanted(at(y + i, zh), 1)
+
+    def first_queries(i):
+        sq[i] = wanted(ahead(i), 0)
+
+    loop(NZ, NY * NZ, second_queries)
+    loop(1, NCTX, first_queries)
     pl.semaphore_wait(barrier, NCTX + NDP - 2)
 
     def pre_z(i):
@@ -181,25 +231,11 @@
     def q2_copy(i):
         return remote(sq2.at[i], rq2.at[i], sq2_s.at[i], rq2_s.at[i], at(y + i, z))
 
-    def wanted(h, second):
-        return qt_ref[jnp.maximum(table[h, 0, second * NCTX + me], 0)]
-
-    def relay_queries(i):
-        def one(zh):
-            sq2[i, zh] = wanted(at(y + i, zh), 1)
-
-        loop(0, NZ, one)
-        q2_copy(i).start()
-
     def q_copy(i):
         return remote(sq.at[i], rq.at[i], sq_s.at[i], rq_s.at[i], ahead(i))
 
-    def send_queries(i):
-        sq[i] = wanted(ahead(i), 0)
-        q_copy(i).start()
-
-    loop(1, NY, relay_queries)
-    loop(1, NCTX, send_queries)
+    loop(1, NY, lambda i: q2_copy(i).start())
+    loop(1, NCTX, lambda i: q_copy(i).start())
     rq[0] = wanted(me, 0)
 
     def own_relay(zh):
@@ -214,21 +250,20 @@
     t = lax.broadcasted_iota(jnp.int32, (16, 128), 0)
     causal = t <= lax.broadcasted_iota(jnp.int32, (16, 128), 1) % 4
 
+    new16[...] = jnp.zeros_like(new16)
+
     def fresh(r):
+        new16[0:4, :] = fresh_ref[r].astype(jnp.float32)
         for h in range(2):
             ln = pl.ds(h * 128, 128)
-            keys = fresh_ref[r, :, pl.ds(h * 512, 512)]
-            values = [fresh_ref[r, :, pl.ds(1024 + (4 * h + k) * 128, 128)] for k in range(4)]
+            keys = new16[:, pl.ds(h * 512, 512)].astype(jnp.bfloat16)
+            values = [new16[:, pl.ds(1024 + (4 * h + k) * 128, 128)].astype(jnp.bfloat16) for k in range(4)]
             m, l, o = group_half(keys, values, qt_ref[r, :, ln], causal)
             big[r, :, ln] = m
             tot[r, :, ln] = l
             acc[r, :, ln] = o
 
     loop(0, 16, fresh)
-
-    loop(1, NY, lambda i: pre_y(i).wait())
-    loop(1, NDP, lambda i: pre_dp(i).start())
-    pre2[0] = pre1[...]
 
     page_load.wait()
 
@@ -302,8 +337,8 @@
     def u_copy(i, zh):
         return remote(su.at[i, zh], ru.at[i, zh], su_s.at[i, zh], ru_s.at[i, zh], at(y + i, z))
 
-    def ul_copy(i, zh):
-        return remote(sul.at[i, zh], rul.at[i, zh], sul_s.at[i, zh], rul_s.at[i, zh], at(y + i, z))
+    def ul_copy(i):
+        return remote(sul.at[i], rul.at[i], sul_s.at[i], rul_s.at[i], at(y + i, z))
 
     def hand_on(d):
         zh = (z + d) % NZ
@@ -322,12 +357,15 @@
             else:
                 su[i, zh] = o
                 sul[i, zh] = l
-                ul_copy(i, zh).start()
                 u_copy(i, zh).start()
 
     loop(1, RELAY, answer)
     loop(1, NY, lambda i: q2_copy(i).wait())
     loop(1, NZ, pack_send)
+    loop(1, NY, lambda i: pre_y(i).wait())
+    loop(1, NDP, lambda i: pre_dp(i).start())
+    pre2[0] = pre1[...]
+
     pack(0, rpk)
     attend2(0, rp2, rl2)
     loop(RELAY, EARLY, answer)
@@ -411,6 +449,7 @@
 
     hand_on(0)
     loop(1, NZ, relay_back)
+    loop(1, NY, lambda i: ul_copy(i).start())
     loop(TAKEN // 4, NCTX // 4, take)
 
     def merge_second(i, zh):
@@ -419,11 +458,8 @@
         merge([(table[at(y + NY - i, h), 0, NCTX + me], rul.at[i, h], ru.at[i, h]) for h in hs])
 
     def take_second(i):
-        def arrive2(zh):
-            ul_copy(i, zh).wait()
-            u_copy(i, zh).wait()
-
-        loop(0, NZ, arrive2)
+        ul_copy(i).wait()
+        loop(0, NZ, lambda zh: u_copy(i, zh).wait())
         loop(0, max(1, NZ // 4), lambda k: merge_second(i, 4 * k))
 
     loop(0, max(1, NZ // 4), lambda k: merge_second(0, 4 * k))
@@ -462,9 +498,10 @@
             pltpu.VMEM((NDP, NY, NZ, 32, 128), jnp.bfloat16),
             pltpu.VMEM((NCTX * 32, 128), jnp.float32),
             pltpu.VMEM((16, 2 * NCTX * NDP, 128), jnp.bfloat16),
+            pltpu.VMEM((16, 2048), jnp.float32),
             dma((NCTX,)), dma((NCTX,)), dma((NCTX,)), dma((NCTX,)), dma((NCTX,)), dma((NCTX,)),
             dma((NY,)), dma((NY,)), dma((NZ,)), dma((NZ,)), dma((NZ,)), dma((NZ,)), dma((NZ,)), dma((NZ,)),
-            dma((NY, NZ)), dma((NY, NZ)), dma((NY, NZ)), dma((NY, NZ)),
+            dma((NY, NZ)), dma((NY, NZ)), dma((NY,)), dma((NY,)),
             dma((NZ,)), dma((NZ,)), dma((NY,)), dma((NY,)), dma((NDP,)), dma((NDP,)), dma,
         ],
         compiler_params=pltpu.CompilerParams(
@@ -479,31 +516,31 @@
     smem = pl.BlockSpec(memory_space=pltpu.SMEM)
     vmem = pl.BlockSpec(memory_space=pltpu.VMEM)
     dma = pltpu.SemaphoreType.DMA
-    table, own, level = pl.pallas_call(
+    table, own, level, qt, prefix = pl.pallas_call(
         meta_kernel,
         out_shape=[
             jax.ShapeDtypeStruct((NCTX, 1, 128), jnp.int32),
             jax.ShapeDtypeStruct((4, 128), jnp.int32),
             jax.ShapeDtypeStruct((1, 128), jnp.int32),
+            jax.ShapeDtypeStruct((request_count, HD, 256), jnp.bfloat16),
+            jax.ShapeDtypeStruct((32, 128), jnp.bfloat16),
         ],
-        in_specs=[smem] * 3,
-        out_specs=[vmem] * 3,
+        in_specs=[smem] * 3 + [vmem] * 2,
+        out_specs=[vmem] * 5,
         scratch_shapes=[
-            pltpu.VMEM((1, 1, 128), jnp.int32),
             pltpu.VMEM((NDP, 8, 128), jnp.int32),
-            dma((NDP,)), dma((NDP,)), dma((NCTX,)), dma((NCTX,)),
+            pltpu.VMEM((32, 128), jnp.float32),
+            dma((NDP,)), dma((NDP,)), dma((NZ,)), dma((NZ,)), dma((NY,)), dma((NY,)),
         ],
-        compiler_params=pltpu.CompilerParams(collective_id=0, has_side_effects=True),
+        compiler_params=pltpu.CompilerParams(
+            collective_id=0, has_side_effects=True, vmem_limit_bytes=60 * 2**20
+        ),
         name="meta",
-    )(page_owner, page_request, page_fill)
-
-    qt = queries.reshape(request_count, step_count, KVH * G, HD).transpose(0, 3, 2, 1).reshape(request_count, HD, 256)
-    fresh = jnp.pad(new_kv, ((0, 0), (0, 12), (0, 0)))
-    prefix = prefix_kv.reshape(32, 128)
+    )(page_owner.reshape(-1), page_request, page_fill, queries, prefix_kv)
     out = lax.switch(
         level[0, 0],
         [functools.partial(attend_all, cap) for cap in (1, 2, 4)],
-        table, own, prefix_use, qt, kv_pages, fresh, prefix,
+        table, own, prefix_use, qt, kv_pages, new_kv, prefix,
     )
     out = out.reshape(request_count, HD, KVH * G, step_count).transpose(0, 3, 2, 1)
     return out.reshape(request_count, step_count, query_width)

time: 206 us -> 198 us (0.961); the launches traced: 206 us -> 194 us
  local copies, waits for them, and re-layouts: 10.4 us -> 2.88 us
  Pallas kernels: 194 us -> 190 us
    pallas_call x1, Pallas kernels: 174 us -> 169 us  [attend_all(): pl.pallas_call(functools.partial(kernel, cap), out_shape=jax.ShapeDtypeSt...]
    reshape x2 -> x0, local copies, waits for them, and re-layouts: 2.86 us -> none  [the longest x1 2.15 us: body(): queries.reshape(request_count, step_count, KVH * G, HD)]
where the time goes in v3:
time: 198 us; the launch traced here: 194 us
  Pallas kernels  190 us (96%)
  local copies, waits for them, and re-layouts  2.88 us (1%)
    pallas_call x1, Pallas kernels, attend_all(): pl.pallas_call(functools.partial(kernel, cap), out_shape=jax.ShapeDtypeSt...  169 us
    pallas_call x1, Pallas kernels, body(): pl.pallas_call(meta_kernel, out_shape=[jax.ShapeDtypeStruct((NCTX, 1, 128...  21.4 us

profile of v3, /device:TPU:32, one launch (start us, length us, event | category | flops | bytes accessed | tf_op | source)
XLA Modules:
  0.0 194.1 jit_solution(14954219270512988102)
XLA Ops:
  0.0 21.4 %meta.1 = (s32[32,1,128]{2,1,0:T(1,128)S(1)}, s32[4,128]{1,0:T(4,128)S(1)}, s32[1,128]{1,0:T(1,128)}, bf16[16,128,256]{2,1,0:T(8,128)(2,1)S(1)}, bf16[32,128]{1,0:T(8,128)(2,1)S(1)}) custom-call(s32[32]{0:T(128)} %bitcast.9, s32[32]{0:T(128)} %request.1, s32[32]{0:T(128)} %fill.1, bf16[16,4,8192]{2,1,0:T(4,128)(2,1)} %q_ref.1, bf16[2,2048]{1,0:T(2,128)(2,1)} %prefix_ref.1), custom_call_target="tpu_custom_call" | custom-call | tf_op jit(solution)/shard_map/meta/pallas_call | solution.py:519
  22.1 169.2 %conditional.1 = (bf16[16,128,256]{2,1,0:T(8,128)(2,1)S(1)}) conditional(s32[]{:T(128)} %bitcast.1, (s32[32,1,128]{2,1,0:T(1,128)S(1)}, s32[4,128]{1,0:T(4,128)S(1)}, s32[16]{0:T(128)}, bf16[16,128,256]{2,1,0:T(8,128)(2,1)S(1)}, bf16[32,64,2048]{2,1,0:T(8,128)(2,1)}, /*index=5*/bf16[16,4,2048]{2,1,0:T(4,128)(2,1)}, ...), branch_computations={%region_0.0_spmd, %region_1.0_spmd, %region_2.0_spmd} | conditional | bytes 8 | solution.py:540
  22.1 168.7 %attend2.1 = bf16[16,128,256]{2,1,0:T(8,128)(2,1)S(1)} custom-call(s32[32,1,128]{2,1,0:T(1,128)S(1)} %get-tuple-element.58.table, s32[4,128]{1,0:T(4,128)S(1)} %get-tuple-element.59.own, s32[16]{0:T(128)} %get-tuple-element.60.use, bf16[16,128,256]{2,1,0:T(8,128)(2,1)S(1)} %get-tuple-element.61.qt_ref, bf16[32,64,2048]{2,1,0:T(8,128)(2,1)} %get-tuple-element.62.pages_hbm, ...), custom_call_target="tpu_custom_call" | custom-call | tf_op jit(solution)/shard_map/cond/branch_1_fun/attend2/pallas_call | solution.py:485
  191.2 1.1 copy.11
  192.3 0.7 copy.14
  193.0 1.1 reshape.15
